TPU v7x, 32 devices: a whole 2x2x4 slice. The times are simulated.
32 devices in a mesh: row: 8 (over z, x), col: 2 (over core), ka: 2 (over y).
Axes of the slice: x: 2, y: 2, z: 4, core: 2. Of those that a mesh axis runs over, the one named last changes fastest.
Arguments:
- density_rows: bfloat16 [1024, 1024], P('row'), may hold values from -0.1 to 0.9
- response_start: bfloat16 [1024, 1024], P(None, ('col', 'ka')), may hold values from -6 to 6
- density_pattern: int32 [16, 8], replicated, may hold values from 0 to 15
- response_pattern: int32 [16, 8], replicated, may hold values from 0 to 15
Outputs:
- response: bfloat16 [1024, 1024], P('row', ('col', 'ka'))
Inputs may be any that keep to these rules, and one draw needn't show every extreme that they name: `density_pattern`: repeats may occur within a block row. `response_pattern`: repeats may occur within a block row.
All inputs are finite; a program needn't handle non-finite values.
Results may differ from a plain program's by a relative error of at most 0.017.
Values may be sent and summed in bfloat16 or wider, within the bound.
A program may use at most 64 MiB of HBM per device.

v0:
```python
import jax
import jax.numpy as jnp
from jax import lax
from jax.sharding import PartitionSpec as P

BLOCK = 64
ITERS = 2


def block_mask(pattern_list, blocks):
    row_ids = lax.broadcasted_iota(jnp.int32, (blocks, blocks), 0)
    col_ids = lax.broadcasted_iota(jnp.int32, (blocks, blocks), 1)
    listed = jnp.any(pattern_list[:, None, :] == col_ids[:, :, None], axis=2)
    return jnp.logical_or(listed, row_ids == col_ids)


def expand(mask_part, block_width):
    return jnp.repeat(jnp.repeat(mask_part, block_width, axis=0), block_width, axis=1)


def left_product(row_strips, column_share):
    piece = lax.all_gather(column_share, "row", axis=0, tiled=True)
    return tuple(
        (jnp.dot(row_strip, piece, preferred_element_type=jnp.float32) for row_strip in row_strips)
    )


def right_product(row_share, column_strip):
    return jnp.dot(
        lax.all_gather(row_share, ("col", "ka"), axis=1, tiled=True),
        column_strip,
        preferred_element_type=jnp.float32,
    )


def body(density_rows, response_start, density_pattern, response_pattern):
    row_count = density_rows.shape[0]
    full_order = density_rows.shape[1]
    share_cols = response_start.shape[1]
    blocks = full_order // BLOCK
    row_pos = lax.axis_index("row")
    share_pos = lax.axis_index(("col", "ka"))
    density_keep = lax.dynamic_slice_in_dim(
        block_mask(density_pattern, blocks), row_pos * (row_count // BLOCK), row_count // BLOCK, 0
    )
    density = jnp.where(expand(density_keep, BLOCK), density_rows, jnp.zeros_like(density_rows))
    response_keep = lax.dynamic_slice_in_dim(
        block_mask(response_pattern, blocks),
        share_pos * (share_cols // BLOCK),
        share_cols // BLOCK,
        1,
    )
    column_keep = expand(response_keep, BLOCK)
    start_cols = jnp.where(column_keep, response_start, jnp.zeros_like(response_start))
    share_keep = lax.dynamic_slice_in_dim(column_keep, row_pos * row_count, row_count, 0)
    current = lax.dynamic_slice_in_dim(start_cols, row_pos * row_count, row_count, 0)
    density_share = lax.dynamic_slice_in_dim(density, share_pos * share_cols, share_cols, 1)
    density_cols = lax.all_gather(density_share, "row", axis=0, tiled=True)
    for iteration in range(ITERS):
        if iteration == 0:
            forward = jnp.dot(density, start_cols, preferred_element_type=jnp.float32)
        else:
            (forward,) = left_product((density,), current)
        backward = right_product(current, density_cols)
        sym = forward + backward
        qround = sym.astype(jnp.bfloat16)
        (second,) = left_product((density,), forward.astype(jnp.bfloat16))
        tail = right_product(qround, density_cols)
        updated = jnp.where(share_keep, 3.0 * sym - 2.0 * (second + tail), jnp.zeros_like(sym))
        current = updated.astype(jnp.bfloat16)
    return current


def solution(mesh):
    return jax.shard_map(
        body,
        mesh=mesh,
        in_specs=(P("row", None), P(None, ("col", "ka")), P(), P()),
        out_specs=P("row", ("col", "ka")),
        check_vma=False,
    )
```

profile of v0, /device:TPU:0, one launch (start us, length us, event | category | flops | bytes accessed | tf_op | source)
XLA Modules:
  0.0 171.2 jit_solution(14512755909002369446)
XLA Ops:
  0.0 0.0 copy-start.1
  0.0 0.8 copy.17
  0.8 0.1 fusion.8
  0.9 0.1 dynamic-slice_or_fusion
  1.0 0.1 copy.18
  1.1 0.1 broadcast_in_dim.22
  1.2 0.1 reshape.14
  1.3 0.1 broadcast_in_dim.23
  1.4 0.1 copy.24
  1.5 0.0 copy-done.1
  1.5 0.0 copy-start
  1.5 0.2 copy.22
  1.7 0.0 copy-start.2
  1.7 0.7 copy-done.2
  2.4 0.1 copy.20
  2.5 0.1 fusion.9
  2.6 0.1 copy.21
  2.7 0.1 broadcast_in_dim.24
  2.8 0.1 reshape.16
  2.9 0.0 copy-done
  2.9 0.2 copy.23
  3.2 0.3 fusion.10
  3.5 33.0 %all_gather.26 = bf16[1024,256]{1,0:T(8,128)(2,1)S(1)} all-gather(bf16[128,256]{1,0:T(8,128)(2,1)S(1)} %get-tuple-element.5), channel_id=1, replica_groups=mesh['row'=8,'col'=2,'ka'=2] {'row'}, dimensions={0}, use_global_device_ids=true | all-gather | bytes 589824 | tf_op jit(solution)/shard_map/all_gather | solution.py:22
  36.5 0.3 fusion.14
  36.8 10.6 %all_gather.24 = bf16[128,1024]{0,1:T(8,128)(2,1)S(1)} all-gather(bf16[128,256]{0,1:T(8,128)(2,1)S(1)} %constant_dynamic-slice_fusion.1), channel_id=1, replica_groups=mesh['row'=8,'col'=2,'ka'=2] {'col','ka'}, dimensions={1}, use_global_device_ids=true | all-gather | bytes 327680 | tf_op jit(solution)/shard_map/all_gather | solution.py:30
  47.4 27.0 %all_gather.25 = bf16[1024,256]{0,1:T(8,128)(2,1)S(1)} all-gather(bf16[128,256]{0,1:T(8,128)(2,1)S(1)} %constant_dynamic-slice_fusion), channel_id=1, replica_groups=mesh['row'=8,'col'=2,'ka'=2] {'row'}, dimensions={0}, use_global_device_ids=true | all-gather | bytes 589824 | tf_op jit(solution)/shard_map/all_gather | solution.py:58
  74.4 0.3 fusion.11
  74.8 10.6 %all_gather.27 = bf16[128,1024]{1,0:T(8,128)(2,1)S(1)} all-gather(bf16[128,256]{1,0:T(8,128)(2,1)S(1)} %get-tuple-element.7), channel_id=1, replica_groups=mesh['row'=8,'col'=2,'ka'=2] {'col','ka'}, dimensions={1}, use_global_device_ids=true | all-gather | bytes 327680 | tf_op jit(solution)/shard_map/all_gather | solution.py:30
  85.3 0.3 fusion.6
  85.7 31.4 %all_gather.28 = bf16[1024,256]{1,0:T(8,128)(2,1)S(1)} all-gather(bf16[128,256]{1,0:T(8,128)(2,1)S(1)} %fusion.6), channel_id=1, replica_groups=mesh['row'=8,'col'=2,'ka'=2] {'row'}, dimensions={0}, use_global_device_ids=true | all-gather | bytes 589824 | tf_op jit(solution)/shard_map/all_gather | solution.py:22
  117.0 0.3 fusion.12
  117.3 31.2 %all_gather.30 = bf16[1024,256]{1,0:T(8,128)(2,1)S(1)} all-gather(bf16[128,256]{1,0:T(8,128)(2,1)S(1)} %get-tuple-element.9), channel_id=1, replica_groups=mesh['row'=8,'col'=2,'ka'=2] {'row'}, dimensions={0}, use_global_device_ids=true | all-gather | bytes 589824 | tf_op jit(solution)/shard_map/all_gather | solution.py:22
  148.5 0.3 fusion.15
  148.8 10.6 %all_gather.29 = bf16[128,1024]{1,0:T(8,128)(2,1)S(1)} all-gather(bf16[128,256]{1,0:T(8,128)(2,1)S(1)} %fusion.6), channel_id=1, replica_groups=mesh['row'=8,'col'=2,'ka'=2] {'col','ka'}, dimensions={1}, use_global_device_ids=true | all-gather | bytes 327680 | tf_op jit(solution)/shard_map/all_gather | solution.py:30
  159.4 0.3 fusion.13
  159.7 10.6 %all_gather.31 = bf16[128,1024]{1,0:T(8,128)(2,1)S(1)} all-gather(bf16[128,256]{1,0:T(8,128)(2,1)S(1)} %get-tuple-element.11), channel_id=1, replica_groups=mesh['row'=8,'col'=2,'ka'=2] {'col','ka'}, dimensions={1}, use_global_device_ids=true | all-gather | bytes 327680 | tf_op jit(solution)/shard_map/all_gather | solution.py:30
  170.2 0.9 fusion.7
  (7 shorter events, 0.1 us)
Async XLA Ops:
  0.0 1.5 copy-start.1
  1.5 1.4 copy-start
  1.7 0.7 copy-start.2
where the time goes:
time: 171 us
  blocking collectives  165 us (96%)
  matrix products  3.01 us (2%)
  local copies, waits for them, and re-layouts  2.71 us (2%)
    all_gather x3, blocking collectives, left_product(): piece = lax.all_gather(column_share, 'row', axis=0, tiled=True)  95.6 us
    all_gather x4, blocking collectives, right_product(): lax.all_gather(row_share, ('col', 'ka'), axis=1, tiled=True)  42.2 us
    all_gather x1, blocking collectives, body(): density_cols = lax.all_gather(density_share, 'row', axis=0, tiled=True)  27 us

commit v1 on v0

v1 whole, which is shorter than its diff:
```python
import functools

import jax
import jax.numpy as jnp
from jax import lax
from jax.experimental import pallas as pl
from jax.experimental.pallas import tpu as pltpu
from jax.sharding import PartitionSpec as P

BLOCK = 64
ITERS = 2
LANES = 2
MESH = pl.DeviceIdType.MESH


def keep_row(pattern_ref, block_row, first_col, cols):
    listed = pattern_ref[pl.ds(block_row, 1), :]
    col_block = (lax.broadcasted_iota(jnp.int32, (1, cols), 1) + first_col) // BLOCK
    keep = col_block == block_row
    for k in range(listed.shape[1]):
        keep = jnp.logical_or(keep, col_block == listed[:, k : k + 1])
    return keep


def masked(keep, values):
    values = values.astype(jnp.float32)
    return jnp.where(jnp.broadcast_to(keep, values.shape), values, jnp.zeros_like(values))


def dot(a, b):
    return jnp.dot(a, b, preferred_element_type=jnp.float32)


def kernel(
    axes,
    nrow,
    ncol,
    nka,
    density_in,
    start_in,
    dpat,
    rpat,
    out_ref,
    density,
    start,
    fwd,
    sym,
    cols_of,
    rows_of,
    row_send,
    row_recv,
    share_send,
    share_recv,
):
    rows, order = density_in.shape
    share_cols = start_in.shape[1]
    nshare = ncol * nka
    nhi = nrow // LANES
    per_row = rows // BLOCK
    row = lax.axis_index("row")
    col = lax.axis_index("col")
    ka = lax.axis_index("ka")
    share = col * nka + ka
    hi, lo = row // LANES, row % LANES

    def device(r, c, k):
        where = {"row": r, "col": c, "ka": k}
        return tuple(where[name] for name in axes)

    hi_peers = [((hi + d) % nhi) * LANES + lo for d in range(1, nhi)]
    lo_peers = [hi * LANES + (lo + d) % LANES for d in range(1, LANES)]
    share_peers = [(share + d) % nshare for d in range(1, nshare)]

    def own_rows(r):
        return pl.ds(pl.multiple_of(r * rows, rows), rows)

    def row_copy(a, slot, target, sem):
        return pltpu.make_async_remote_copy(
            src_ref=cols_of.at[a, own_rows(slot), :],
            dst_ref=cols_of.at[a, own_rows(slot), :],
            send_sem=row_send.at[a, sem],
            recv_sem=row_recv.at[a, slot],
            device_id=device(target, col, ka),
            device_id_type=MESH,
        )

    def row_start(a):
        started = []
        for i, peer in enumerate(hi_peers + lo_peers):
            copy = row_copy(a, row, peer, i)
            copy.start()
            started.append(copy)
        return started

    def row_relay(a, started):
        sem = len(started)
        for peer in hi_peers:
            row_copy(a, peer, peer, 0).wait_recv()
            for target in lo_peers:
                copy = row_copy(a, peer, target, sem)
                copy.start()
                started.append(copy)
                sem += 1

    def row_finish(a):
        for d in range(nhi):
            for e in range(1, LANES):
                slot = ((hi + d) % nhi) * LANES + (lo + e) % LANES
                row_copy(a, slot, slot, 0).wait_recv()

    def share_copy(a, slot, target, sem):
        return pltpu.make_async_remote_copy(
            src_ref=rows_of.at[a, slot],
            dst_ref=rows_of.at[a, slot],
            send_sem=share_send.at[a, sem],
            recv_sem=share_recv.at[a, slot],
            device_id=device(row, target // nka, target % nka),
            device_id_type=MESH,
        )

    def share_start(a):
        started = []
        for i, peer in enumerate(share_peers):
            copy = share_copy(a, share, peer, i)
            copy.start()
            started.append(copy)
        return started

    def share_finish(a):
        for peer in share_peers:
            share_copy(a, peer, peer, 0).wait_recv()

    def left(a):
        return dot(density[...], cols_of[a])

    def right(a):
        total = None
        for s in range(nshare):
            part = dot(rows_of[a, s], cols_of[0, s * share_cols : (s + 1) * share_cols, :])
            total = part if total is None else total + part
        return total

    barrier = pltpu.get_barrier_semaphore()
    greeted = [device(r, col, ka) for r in hi_peers + lo_peers]
    greeted += [device(row, s // nka, s % nka) for s in share_peers]
    for peer in greeted:
        pl.semaphore_signal(barrier, inc=1, device_id=peer, device_id_type=MESH)

    for i in range(per_row):
        keep = keep_row(dpat, row * per_row + i, 0, order)
        part = slice(i * BLOCK, (i + 1) * BLOCK)
        density[part, :] = masked(keep, density_in[part, :]).astype(jnp.bfloat16)
    share_first = pl.multiple_of(share * share_cols, share_cols)
    cols_of[0, own_rows(row), :] = density[:, pl.ds(share_first, share_cols)]
    pl.semaphore_wait(barrier, len(greeted))
    sent = row_start(0)

    for b in range(order // BLOCK):
        keep = keep_row(rpat, b, share_first, share_cols)
        part = slice(b * BLOCK, (b + 1) * BLOCK)
        start[part, :] = masked(keep, start_in[part, :]).astype(jnp.bfloat16)
    rows_of[0, share] = start[own_rows(row), :]
    sent += share_start(0)
    fwd[...] = dot(density[...], start[...])
    cols_of[1, own_rows(row), :] = fwd[...].astype(jnp.bfloat16)

    d_sent = sent[: nrow // LANES - 1 + LANES - 1]
    relayed = list(d_sent)
    row_relay(0, relayed)
    sent += relayed[len(d_sent) :]
    w_sent = row_start(1)
    row_finish(0)

    a_row, a_share = 1, 0
    for iteration in range(ITERS):
        share_finish(a_share)
        sym[...] = fwd[...] + right(a_share)
        rows_of[a_share + 1, share] = sym[...].astype(jnp.bfloat16)
        sent += share_start(a_share + 1)
        row_relay(a_row, w_sent)
        sent += w_sent
        row_finish(a_row)
        second = left(a_row)
        share_finish(a_share + 1)
        total = 3.0 * sym[...] - 2.0 * (second + right(a_share + 1))
        for i in range(per_row):
            keep = keep_row(rpat, row * per_row + i, share_first, share_cols)
            part = slice(i * BLOCK, (i + 1) * BLOCK)
            updated = masked(keep, total[part, :]).astype(jnp.bfloat16)
            if iteration == ITERS - 1:
                out_ref[part, :] = updated
            else:
                rows_of[a_share + 2, share, part, :] = updated
        if iteration == ITERS - 1:
            break
        a_row, a_share = a_row + 1, a_share + 2
        cols_of[a_row, own_rows(row), :] = rows_of[a_share, share]
        x_sent = row_start(a_row)
        sent += share_start(a_share)
        row_relay(a_row, x_sent)
        sent += x_sent
        row_finish(a_row)
        fwd[...] = left(a_row)
        a_row += 1
        cols_of[a_row, own_rows(row), :] = fwd[...].astype(jnp.bfloat16)
        w_sent = row_start(a_row)

    for copy in sent:
        copy.wait_send()


def solution(mesh):
    nrow, ncol, nka = (mesh.shape[name] for name in ("row", "col", "ka"))
    nshare = ncol * nka

    def body(density_rows, response_start, density_pattern, response_pattern):
        rows, order = density_rows.shape
        share_cols = response_start.shape[1]
        row_sends = nrow // LANES - 1 + LANES - 1 + (nrow // LANES - 1) * (LANES - 1)
        vmem = pl.BlockSpec(memory_space=pltpu.VMEM)
        return pl.pallas_call(
            functools.partial(kernel, mesh.axis_names, nrow, ncol, nka),
            out_shape=jax.ShapeDtypeStruct((rows, share_cols), jnp.bfloat16),
            in_specs=[vmem] * 4,
            out_specs=vmem,
            scratch_shapes=[
                pltpu.VMEM((rows, order), jnp.bfloat16),
                pltpu.VMEM((order, share_cols), jnp.bfloat16),
                pltpu.VMEM((rows, share_cols), jnp.float32),
                pltpu.VMEM((rows, share_cols), jnp.float32),
                pltpu.VMEM((2 * ITERS, order, share_cols), jnp.bfloat16),
                pltpu.VMEM((2 * ITERS, nshare, rows, share_cols), jnp.bfloat16),
                pltpu.SemaphoreType.DMA((2 * ITERS, row_sends)),
                pltpu.SemaphoreType.DMA((2 * ITERS, nrow)),
                pltpu.SemaphoreType.DMA((2 * ITERS, nshare)),
                pltpu.SemaphoreType.DMA((2 * ITERS, nshare)),
            ],
            compiler_params=pltpu.CompilerParams(
                collective_id=0, has_side_effects=True, vmem_limit_bytes=40 * 1024 * 1024
            ),
            cost_estimate=pl.CostEstimate(
                flops=8 * ITERS * rows * order * share_cols,
                bytes_accessed=2 * order * (rows + share_cols),
                transcendentals=0,
            ),
        )(density_rows, response_start, density_pattern, response_pattern)

    return jax.shard_map(
        body,
        mesh=mesh,
        in_specs=(P("row", None), P(None, ("col", "ka")), P(), P()),
        out_specs=P("row", ("col", "ka")),
        check_vma=False,
    )
```

time: 171 us -> 48.8 us (0.29)
  blocking collectives: 165 us -> 0 us
  Pallas kernels: 0 us -> 44.5 us
  matrix products: 3.01 us -> 0 us
    all_gather x8 -> x0, blocking collectives: 165 us -> none  [the longest x3 95.6 us: left_product(): piece = lax.all_gather(column_share, 'row', axis=0, tiled=True)]
    pallas_call x0 -> x1, Pallas kernels: none -> 44.5 us  [body(): pl.pallas_call(functools.partial(kernel, mesh.axis_names, nrow, ncol, nka...]
    dot_general x8 -> x0, matrix products: 3.01 us -> none  [the longest x4 1.89 us: right_product(): jnp.dot(lax.all_gather(row_share, ('col', 'ka'), axis=1, tiled=True), col...]
    unnamed x11 -> x9, local copies, waits for them, and re-layouts: 2.05 us -> 3.47 us
where the time goes in v1:
time: 48.8 us; the launch traced here: 48 us
  Pallas kernels  44.5 us (91%)
  local copies, waits for them, and re-layouts  3.47 us (7%)
    pallas_call x1, Pallas kernels, body(): pl.pallas_call(functools.partial(kernel, mesh.axis_names, nrow, ncol, nka...  44.5 us
    unnamed x9, local copies, waits for them, and re-layouts  3.47 us

profile of v1, /device:TPU:0, one launch (start us, length us, event | category | flops | bytes accessed | tf_op | source)
XLA Modules:
  0.0 48.0 jit_solution(10313225626551787436)
XLA Ops:
  0.0 0.0 copy-start.2
  0.0 0.8 %copy.5.dpat = s32[16,8]{1,0:T(8,128)S(1)} copy(s32[16,8]{0,1:T(8,128)} %param.6) | data formatting | bytes 1024 | tf_op args[2]
  0.8 0.0 copy-done.2
  0.8 0.1 copy.6.rpat
  0.8 0.0 copy-start
  0.8 1.0 %copy-done = bf16[1024,256]{1,0:T(8,128)(2,1)S(1)} copy-done((bf16[1024,256]{1,0:T(8,128)(2,1)S(1)}, bf16[1024,256]{1,0:T(8,128)(2,1)}, u32[]{:S(2)}) %copy-start) | copy-done | bytes 524312
  1.9 0.0 copy-start.1
  1.9 0.9 %copy-done.1 = bf16[128,1024]{1,0:T(8,128)(2,1)S(1)} copy-done((bf16[128,1024]{1,0:T(8,128)(2,1)S(1)}, bf16[128,1024]{1,0:T(8,128)(2,1)}, u32[]{:S(2)}) %copy-start.1) | copy-done | bytes 262168
  2.8 44.5 %shard_map.46 = bf16[128,256]{1,0:T(8,128)(2,1)S(1)} custom-call(bf16[128,1024]{1,0:T(8,128)(2,1)S(1)} %copy-done.1, bf16[1024,256]{1,0:T(8,128)(2,1)S(1)} %copy-done, s32[16,8]{1,0:T(8,128)S(1)} %copy.5.dpat, s32[16,8]{1,0:T(8,128)S(1)} %copy.6.rpat), custom_call_target="tpu_custom_call" | custom-call | flops 536870912 | bytes 786432 | tf_op jit(solution)/shard_map/pallas_call | solution.py:221
  47.4 0.6 %copy.8 = bf16[128,256]{1,0:T(8,128)(2,1)} copy(bf16[128,256]{1,0:T(8,128)(2,1)S(1)} %shard_map.46) | data formatting | bytes 131072
Async XLA Ops:
  0.0 0.8 %copy-start.2 = (s32[16,8]{0,1:T(8,128)S(1)}, s32[16,8]{0,1:T(8,128)}, u32[]{:S(2)}) copy-start(s32[16,8]{0,1:T(8,128)} %param.7) | copy-start | bytes 1540
  0.8 1.0 %copy-start = (bf16[1024,256]{1,0:T(8,128)(2,1)S(1)}, bf16[1024,256]{1,0:T(8,128)(2,1)}, u32[]{:S(2)}) copy-start(bf16[1024,256]{1,0:T(8,128)(2,1)} %start_in.1) | copy-start | bytes 1572868
  1.9 0.9 %copy-start.1 = (bf16[128,1024]{1,0:T(8,128)(2,1)S(1)}, bf16[128,1024]{1,0:T(8,128)(2,1)}, u32[]{:S(2)}) copy-start(bf16[128,1024]{1,0:T(8,128)(2,1)} %density_in.1) | copy-start | bytes 786436

commit v2 on v1

--- a/solution.py
+++ b/solution.py
@@ -209,6 +209,280 @@
         copy.wait_send()
 
 
+SENDS = 96
+
+
+def whole_kernel(
+    axes,
+    nrow,
+    ncol,
+    nka,
+    density_in,
+    start_in,
+    dpat,
+    rpat,
+    out_ref,
+    d_stage,
+    x_stage,
+    df,
+    xf,
+    sym,
+    squares,
+    sym_b,
+    squares_b,
+    x1,
+    f1,
+    strips,
+    send,
+    drecv,
+    xrecv,
+    srecv,
+    local,
+):
+    rows, order = density_in.shape
+    cols = start_in.shape[1]
+    nshare = ncol * nka
+    nhi = nrow // LANES
+    per_row = rows // BLOCK
+    row = lax.axis_index("row")
+    col = lax.axis_index("col")
+    ka = lax.axis_index("ka")
+    mine = col * nka + ka
+    core_share = (1 - col) * nka + ka
+    y_share = col * nka + (1 - ka)
+    diag_share = (1 - col) * nka + (1 - ka)
+    hi, lo = row // LANES, row % LANES
+
+    def device(r, c, k):
+        where = {"row": r, "col": c, "ka": k}
+        return tuple(where[name] for name in axes)
+
+    z_rows = [((hi + d) % nhi) * LANES + lo for d in (1, nhi - 1, *range(2, nhi - 1))]
+    x_row = hi * LANES + 1 - lo
+    x_rows = [x_row] + [(z // LANES) * LANES + 1 - lo for z in z_rows]
+    z_devices = [device(r, col, ka) for r in z_rows]
+    x_device = device(x_row, col, ka)
+    y_device = device(row, col, 1 - ka)
+    core_device = device(row, 1 - col, ka)
+    greeted = z_devices + [x_device, y_device, core_device]
+
+    d_copy = pltpu.make_async_copy(density_in, d_stage, local.at[0])
+    d_copy.start()
+    x_copy = pltpu.make_async_copy(start_in, x_stage, local.at[1])
+    x_copy.start()
+    barrier = pltpu.get_barrier_semaphore()
+    for peer in greeted:
+        pl.semaphore_signal(barrier, inc=1, device_id=peer, device_id_type=MESH)
+
+    def block(ref, s, r):
+        return ref.at[s, pl.ds(pl.multiple_of(r * rows, rows), rows), :]
+
+    sent = []
+
+    def push(ref, sem, target):
+        copy = pltpu.make_async_remote_copy(
+            src_ref=ref,
+            dst_ref=ref,
+            send_sem=send.at[len(sent)],
+            recv_sem=sem,
+            device_id=target,
+            device_id_type=MESH,
+        )
+        copy.start()
+        sent.append(copy)
+
+    def arrived(ref, sem):
+        pltpu.make_async_remote_copy(
+            src_ref=ref,
+            dst_ref=ref,
+            send_sem=send.at[0],
+            recv_sem=sem,
+            device_id=core_device,
+            device_id_type=MESH,
+        ).wait_recv()
+
+    def push_d(s, r, *targets):
+        for target in targets:
+            push(block(df, s, r), drecv.at[s, r], target)
+
+    def push_x(s, r, *targets):
+        for target in targets:
+            push(block(xf, s, r), xrecv.at[s, r], target)
+
+    def wait_d(s, r):
+        arrived(block(df, s, r), drecv.at[s, r])
+
+    def wait_x(s, r):
+        arrived(block(xf, s, r), xrecv.at[s, r])
+
+    def share_rows(s):
+        return pl.ds(pl.multiple_of(s * cols, cols), cols)
+
+    def left_add(total, s, right_ref, lead):
+        part = right_ref[(*lead, share_rows(s), slice(None))]
+        total[...] += dot(df[s], part)
+
+    def left_parts(s):
+        left_add(sym, s, xf, (mine,))
+        left_add(squares, s, df, (mine,))
+
+    def right_parts(s):
+        sym[...] += dot(xf[s], df[mine, share_rows(s), :])
+
+    own = pl.ds(pl.multiple_of(row * rows, rows), rows)
+    first_col = pl.multiple_of(mine * cols, cols)
+
+    d_copy.wait()
+    for i in range(per_row):
+        keep = keep_row(dpat, row * per_row + i, 0, order)
+        kept = masked(keep, d_stage[i * BLOCK : (i + 1) * BLOCK, :]).astype(jnp.bfloat16)
+        where = pl.ds(pl.multiple_of(row * rows + i * BLOCK, BLOCK), BLOCK)
+        for s in range(nshare):
+            df[s, where, :] = kept[:, s * cols : (s + 1) * cols]
+    x_copy.wait()
+    for b in range(order // BLOCK):
+        keep = keep_row(rpat, b, first_col, cols)
+        part = slice(b * BLOCK, (b + 1) * BLOCK)
+        xf[mine, part, :] = masked(keep, x_stage[part, :]).astype(jnp.bfloat16)
+    pl.semaphore_wait(barrier, len(greeted))
+
+    push_x(mine, row, y_device)
+    push_d(mine, row, *z_devices, x_device)
+    push(xf.at[mine], xrecv.at[mine, 0], core_device)
+    sym[...] = jnp.zeros_like(sym)
+    squares[...] = jnp.zeros_like(squares)
+    wait_x(y_share, row)
+    push_x(y_share, row, *z_devices, x_device, core_device)
+    for z in z_rows:
+        wait_d(mine, z)
+        push_d(mine, z, x_device, y_device, core_device)
+    for i, z in enumerate(z_rows):
+        wait_d(mine, x_rows[i])
+        push_d(mine, x_rows[i], y_device, core_device)
+        wait_x(y_share, z)
+        push_x(y_share, z, x_device, core_device)
+    for r in x_rows[nhi - 1 :]:
+        wait_d(mine, r)
+        push_d(mine, r, y_device, core_device)
+    left_parts(mine)
+    right_parts(mine)
+    arrived(xf.at[core_share], xrecv.at[core_share, 0])
+    right_parts(core_share)
+    others = z_rows + x_rows
+    for i, r in enumerate(others):
+        wait_d(y_share, r)
+        push_d(y_share, r, core_device)
+        if i < nhi:
+            wait_x(y_share, x_rows[i])
+            push_x(y_share, x_rows[i], core_device)
+    right_parts(y_share)
+    left_parts(y_share)
+    for r in others:
+        wait_d(core_share, r)
+    left_parts(core_share)
+    for r in [row] + others:
+        wait_x(diag_share, r)
+    right_parts(diag_share)
+    for r in others:
+        wait_d(diag_share, r)
+    left_parts(diag_share)
+
+    sym_b[...] = sym[...].astype(jnp.bfloat16)
+    squares_b[...] = squares[...].astype(jnp.bfloat16)
+    twice = None
+    for s in range(nshare):
+        at = slice(s * cols, (s + 1) * cols)
+        part = dot(df[s], sym_b[at, :]) + dot(xf[s], squares_b[at, :])
+        twice = part if twice is None else twice + part
+    sym[...] = 3.0 * sym[...] - 2.0 * twice
+    for b in range(order // BLOCK):
+        keep = keep_row(rpat, b, first_col, cols)
+        part = slice(b * BLOCK, (b + 1) * BLOCK)
+        x1[part, :] = masked(keep, sym[part, :]).astype(jnp.bfloat16)
+
+    strips[0, mine] = x1[own, :]
+
+    def push_strip(a, s, *targets):
+        for target in targets:
+            push(strips.at[a, s], srecv.at[a, s], target)
+
+    push_strip(0, mine, y_device, core_device)
+
+    def density_dot(ref):
+        total = None
+        for s in range(nshare):
+            part = dot(df[s, own, :], ref[s * cols : (s + 1) * cols, :])
+            total = part if total is None else total + part
+        return total
+
+    forward = density_dot(x1)
+    strips[1, mine] = forward.astype(jnp.bfloat16)
+    push_strip(1, mine, y_device, core_device)
+    full = None
+    for s in range(nshare):
+        part = dot(df[s], x1[s * cols : (s + 1) * cols, :])
+        full = part if full is None else full + part
+    f1[...] = full.astype(jnp.bfloat16)
+    result = 3.0 * forward - 2.0 * density_dot(f1)
+    for a in range(2):
+        arrived(strips.at[a, y_share], srecv.at[a, y_share])
+        push_strip(a, y_share, core_device)
+    for s in (core_share, diag_share):
+        for a in range(2):
+            arrived(strips.at[a, s], srecv.at[a, s])
+    for s in range(nshare):
+        at = slice(s * cols, (s + 1) * cols)
+        d_part = df[mine, at, :]
+        result += 3.0 * dot(strips[0, s], d_part)
+        result -= 2.0 * (dot(strips[1, s], d_part) + dot(strips[0, s], squares_b[at, :]))
+    for i in range(per_row):
+        keep = keep_row(rpat, row * per_row + i, first_col, cols)
+        part = slice(i * BLOCK, (i + 1) * BLOCK)
+        out_ref[part, :] = masked(keep, result[part, :]).astype(jnp.bfloat16)
+
+    for copy in sent:
+        copy.wait_send()
+
+
+def whole_call(axes, nrow, ncol, nka, rows, order, cols):
+    nshare = ncol * nka
+    vmem = pl.BlockSpec(memory_space=pltpu.VMEM)
+    hbm = pl.BlockSpec(memory_space=pl.ANY)
+    bf16, f32 = jnp.bfloat16, jnp.float32
+    return pl.pallas_call(
+        functools.partial(whole_kernel, axes, nrow, ncol, nka),
+        out_shape=jax.ShapeDtypeStruct((rows, cols), bf16),
+        in_specs=[hbm, hbm, vmem, vmem],
+        out_specs=vmem,
+        scratch_shapes=[
+            pltpu.VMEM((rows, order), bf16),
+            pltpu.VMEM((order, cols), bf16),
+            pltpu.VMEM((nshare, order, cols), bf16),
+            pltpu.VMEM((nshare, order, cols), bf16),
+            pltpu.VMEM((order, cols), f32),
+            pltpu.VMEM((order, cols), f32),
+            pltpu.VMEM((order, cols), bf16),
+            pltpu.VMEM((order, cols), bf16),
+            pltpu.VMEM((order, cols), bf16),
+            pltpu.VMEM((order, cols), bf16),
+            pltpu.VMEM((2, nshare, rows, cols), bf16),
+            pltpu.SemaphoreType.DMA((SENDS,)),
+            pltpu.SemaphoreType.DMA((nshare, nrow)),
+            pltpu.SemaphoreType.DMA((nshare, nrow)),
+            pltpu.SemaphoreType.DMA((2, nshare)),
+            pltpu.SemaphoreType.DMA((2,)),
+        ],
+        compiler_params=pltpu.CompilerParams(
+            collective_id=1, has_side_effects=True, vmem_limit_bytes=40 * 1024 * 1024
+        ),
+        cost_estimate=pl.CostEstimate(
+            flops=13 * order * order * cols,
+            bytes_accessed=2 * order * (rows + cols),
+            transcendentals=0,
+        ),
+    )
+
+
 def solution(mesh):
     nrow, ncol, nka = (mesh.shape[name] for name in ("row", "col", "ka"))
     nshare = ncol * nka
@@ -216,6 +490,10 @@
     def body(density_rows, response_start, density_pattern, response_pattern):
         rows, order = density_rows.shape
         share_cols = response_start.shape[1]
+        if ncol == 2 and nka == 2 and nrow == 8 and order <= 1024:
+            return whole_call(mesh.axis_names, nrow, ncol, nka, rows, order, share_cols)(
+                density_rows, response_start, density_pattern, response_pattern
+            )
         row_sends = nrow // LANES - 1 + LANES - 1 + (nrow // LANES - 1) * (LANES - 1)
         vmem = pl.BlockSpec(memory_space=pltpu.VMEM)
         return pl.pallas_call(

time: 48.8 us -> 38.1 us (0.78)
  Pallas kernels: 44.5 us -> 34 us
    pallas_call x1, Pallas kernels: 44.5 us -> 34 us  [body(): whole_call(mesh.axis_names, nrow, ncol, nka, rows, order, share_cols)]
where the time goes in v2:
time: 38.1 us; the launch traced here: 37.5 us
  Pallas kernels  34 us (89%)
  local copies, waits for them, and re-layouts  3.47 us (9%)
    pallas_call x1, Pallas kernels, body(): whole_call(mesh.axis_names, nrow, ncol, nka, rows, order, share_cols)  34 us
    unnamed x9, local copies, waits for them, and re-layouts  3.47 us

profile of v2, /device:TPU:0, one launch (start us, length us, event | category | flops | bytes accessed | tf_op | source)
XLA Modules:
  0.0 37.5 jit_solution(13983078702787085172)
XLA Ops:
  0.0 0.0 copy-start.2
  0.0 0.8 %copy.5.dpat = s32[16,8]{1,0:T(8,128)S(1)} copy(s32[16,8]{0,1:T(8,128)} %param.6) | data formatting | bytes 1024 | tf_op args[2]
  0.8 0.0 copy-done.2
  0.8 0.1 copy.6.rpat
  0.8 0.0 copy-start
  0.8 1.0 %copy-done = bf16[1024,256]{1,0:T(8,128)(2,1)S(1)} copy-done((bf16[1024,256]{1,0:T(8,128)(2,1)S(1)}, bf16[1024,256]{1,0:T(8,128)(2,1)}, u32[]{:S(2)}) %copy-start) | copy-done | bytes 524312
  1.9 0.0 copy-start.1
  1.9 0.9 %copy-done.1 = bf16[128,1024]{1,0:T(8,128)(2,1)S(1)} copy-done((bf16[128,1024]{1,0:T(8,128)(2,1)S(1)}, bf16[128,1024]{1,0:T(8,128)(2,1)}, u32[]{:S(2)}) %copy-start.1) | copy-done | bytes 262168
  2.8 34.0 %shard_map.46 = bf16[128,256]{1,0:T(8,128)(2,1)S(1)} custom-call(bf16[128,1024]{1,0:T(8,128)(2,1)S(1)} %copy-done.1, bf16[1024,256]{1,0:T(8,128)(2,1)S(1)} %copy-done, s32[16,8]{1,0:T(8,128)S(1)} %copy.5.dpat, s32[16,8]{1,0:T(8,128)S(1)} %copy.6.rpat), custom_call_target="tpu_custom_call" | custom-call | flops 3489660928 | bytes 786432 | tf_op jit(solution)/shard_map/pallas_call | solution.py:494
  36.8 0.6 %copy.8 = bf16[128,256]{1,0:T(8,128)(2,1)} copy(bf16[128,256]{1,0:T(8,128)(2,1)S(1)} %shard_map.46) | data formatting | bytes 131072
Async XLA Ops:
  0.0 0.8 %copy-start.2 = (s32[16,8]{0,1:T(8,128)S(1)}, s32[16,8]{0,1:T(8,128)}, u32[]{:S(2)}) copy-start(s32[16,8]{0,1:T(8,128)} %param.7) | copy-start | bytes 1540
  0.8 1.0 %copy-start = (bf16[1024,256]{1,0:T(8,128)(2,1)S(1)}, bf16[1024,256]{1,0:T(8,128)(2,1)}, u32[]{:S(2)}) copy-start(bf16[1024,256]{1,0:T(8,128)(2,1)} %start_in.1) | copy-start | bytes 1572868
  1.9 0.9 %copy-start.1 = (bf16[128,1024]{1,0:T(8,128)(2,1)S(1)}, bf16[128,1024]{1,0:T(8,128)(2,1)}, u32[]{:S(2)}) copy-start(bf16[128,1024]{1,0:T(8,128)(2,1)} %density_in.1) | copy-start | bytes 786436

commit v3 on v2

--- a/solution.py
+++ b/solution.py
@@ -369,6 +369,9 @@
     arrived(xf.at[core_share], xrecv.at[core_share, 0])
     right_parts(core_share)
     others = z_rows + x_rows
+    for r in others:
+        wait_d(core_share, r)
+    left_parts(core_share)
     for i, r in enumerate(others):
         wait_d(y_share, r)
         push_d(y_share, r, core_device)
@@ -377,9 +380,6 @@
             push_x(y_share, x_rows[i], core_device)
     right_parts(y_share)
     left_parts(y_share)
-    for r in others:
-        wait_d(core_share, r)
-    left_parts(core_share)
     for r in [row] + others:
         wait_x(diag_share, r)
     right_parts(diag_share)
@@ -424,17 +424,22 @@
         full = part if full is None else full + part
     f1[...] = full.astype(jnp.bfloat16)
     result = 3.0 * forward - 2.0 * density_dot(f1)
+    def share_terms(s):
+        at = share_rows(s)
+        d_part = df[mine, at, :]
+        start_part = dot(strips[0, s], d_part)
+        rest = dot(strips[1, s], d_part) + dot(strips[0, s], squares_b[at, :])
+        return 3.0 * start_part - 2.0 * rest
+
+    result += share_terms(mine)
     for a in range(2):
-        arrived(strips.at[a, y_share], srecv.at[a, y_share])
-        push_strip(a, y_share, core_device)
-    for s in (core_share, diag_share):
+        arrived(strips.at[a, core_share], srecv.at[a, core_share])
+    result += share_terms(core_share)
+    for s, targets in ((y_share, (core_device,)), (diag_share, ())):
         for a in range(2):
             arrived(strips.at[a, s], srecv.at[a, s])
-    for s in range(nshare):
-        at = slice(s * cols, (s + 1) * cols)
-        d_part = df[mine, at, :]
-        result += 3.0 * dot(strips[0, s], d_part)
-        result -= 2.0 * (dot(strips[1, s], d_part) + dot(strips[0, s], squares_b[at, :]))
+            push_strip(a, s, *targets)
+        result += share_terms(s)
     for i in range(per_row):
         keep = keep_row(rpat, row * per_row + i, first_col, cols)
         part = slice(i * BLOCK, (i + 1) * BLOCK)

time: 38.1 us -> 37.9 us (level)
  no operation moved by 1% of the time
where the time goes in v3:
time: 37.9 us; the launch traced here: 37.5 us
  Pallas kernels  34 us (90%)
  local copies, waits for them, and re-layouts  3.47 us (9%)
    pallas_call x1, Pallas kernels, body(): whole_call(mesh.axis_names, nrow, ncol, nka, rows, order, share_cols)  34 us
    unnamed x9, local copies, waits for them, and re-layouts  3.47 us

profile of v3, /device:TPU:0, one launch (start us, length us, event | category | flops | bytes accessed | tf_op | source)
XLA Modules:
  0.0 37.5 jit_solution(8081000130220319777)
XLA Ops:
  0.0 0.0 copy-start.2
  0.0 0.8 %copy.5.dpat = s32[16,8]{1,0:T(8,128)S(1)} copy(s32[16,8]{0,1:T(8,128)} %param.6) | data formatting | bytes 1024 | tf_op args[2]
  0.8 0.0 copy-done.2
  0.8 0.1 copy.6.rpat
  0.8 0.0 copy-start
  0.8 1.0 %copy-done = bf16[1024,256]{1,0:T(8,128)(2,1)S(1)} copy-done((bf16[1024,256]{1,0:T(8,128)(2,1)S(1)}, bf16[1024,256]{1,0:T(8,128)(2,1)}, u32[]{:S(2)}) %copy-start) | copy-done | bytes 524312
  1.9 0.0 copy-start.1
  1.9 0.9 %copy-done.1 = bf16[128,1024]{1,0:T(8,128)(2,1)S(1)} copy-done((bf16[128,1024]{1,0:T(8,128)(2,1)S(1)}, bf16[128,1024]{1,0:T(8,128)(2,1)}, u32[]{:S(2)}) %copy-start.1) | copy-done | bytes 262168
  2.8 34.0 %shard_map.46 = bf16[128,256]{1,0:T(8,128)(2,1)S(1)} custom-call(bf16[128,1024]{1,0:T(8,128)(2,1)S(1)} %copy-done.1, bf16[1024,256]{1,0:T(8,128)(2,1)S(1)} %copy-done, s32[16,8]{1,0:T(8,128)S(1)} %copy.5.dpat, s32[16,8]{1,0:T(8,128)S(1)} %copy.6.rpat), custom_call_target="tpu_custom_call" | custom-call | flops 3489660928 | bytes 786432 | tf_op jit(solution)/shard_map/pallas_call | solution.py:499
  36.8 0.6 %copy.8 = bf16[128,256]{1,0:T(8,128)(2,1)} copy(bf16[128,256]{1,0:T(8,128)(2,1)S(1)} %shard_map.46) | data formatting | bytes 131072
Async XLA Ops:
  0.0 0.8 %copy-start.2 = (s32[16,8]{0,1:T(8,128)S(1)}, s32[16,8]{0,1:T(8,128)}, u32[]{:S(2)}) copy-start(s32[16,8]{0,1:T(8,128)} %param.7) | copy-start | bytes 1540
  0.8 1.0 %copy-start = (bf16[1024,256]{1,0:T(8,128)(2,1)S(1)}, bf16[1024,256]{1,0:T(8,128)(2,1)}, u32[]{:S(2)}) copy-start(bf16[1024,256]{1,0:T(8,128)(2,1)} %start_in.1) | copy-start | bytes 1572868
  1.9 0.9 %copy-start.1 = (bf16[128,1024]{1,0:T(8,128)(2,1)S(1)}, bf16[128,1024]{1,0:T(8,128)(2,1)}, u32[]{:S(2)}) copy-start(bf16[128,1024]{1,0:T(8,128)(2,1)} %density_in.1) | copy-start | bytes 786436
